TPU v7x, 32 devices: a whole 2x2x4 slice. The times are simulated.
32 devices in a mesh: seq: 8 (over z, x), head: 4 (over y, core).
Axes of the slice: x: 2, y: 2, z: 4, core: 2. Of those that a mesh axis runs over, the one named last changes fastest.
Arguments:
- token_values: bfloat16 [2048, 5120], P('seq', 'head'), may hold values from -6 to 6
- gate_values: bfloat16 [2048, 5120], P('seq', 'head'), may hold values from -30 to 30
- state_in: bfloat16 [2048, 128], P('seq'), may hold values from -0.5 to 0.5
- state_out: bfloat16 [2048, 128], P('seq'), may hold values from -6 to 6
- step_size: float32 [2048, 80], P('seq', 'head'), may hold values from 0.02 to 0.2
- log_decay: float32 [2048, 80], P('seq', 'head'), may hold values from -1 to 0
- level_weight: bfloat16 [2048, 80, 12], P('seq', 'head'), may hold values from 0.25 to 2
- skip_weight: float32 [80], P('head'), may hold values from 0.5 to 1.5
- norm_gain: float32 [5120], P('head'), may hold values from 0.1 to 1.9
- out_weight: bfloat16 [5120, 2560], P('head'), may hold values from -0.078125 to 0.078125
Outputs:
- layer_out: bfloat16 [2048, 2560], P(('seq', 'head'))
All inputs are finite; a program needn't handle non-finite values.
Results may differ from a plain program's by a relative error of at most 0.014.
Values may be sent and summed in bfloat16 or wider, within the bound.
A program may use at most 64 MiB of HBM per device.

v0:
```python
import jax
import jax.numpy as jnp
from jax import lax
from jax.sharding import PartitionSpec as P

H = 80
P_SIZE = 64
N = 128
STRETCH_BITS = 6
STRETCH = 64


EPSILON = 1e-05
HIGH = lax.Precision.HIGHEST


def partner_2(value, axis, distance):
    mask = 2**distance
    pairs = [(source, source ^ mask) for source in range(lax.axis_size(axis))]
    return lax.ppermute(value, axis, pairs)


def bit_count(values, bit_width):
    counted = jnp.zeros(values.shape, jnp.int32)
    for shift in range(bit_width):
        counted = counted + (values >= 1 << shift).astype(jnp.int32)
    return counted


def stretch_levels():
    inside = jnp.arange(STRETCH, dtype=jnp.int32)
    later = inside[:, None]
    earlier = inside[None, :]
    causal = earlier <= later
    levels = bit_count(jnp.bitwise_xor(later, earlier), STRETCH_BITS)
    onehot = (
        levels[:, :, None] == jnp.arange(STRETCH_BITS + 1, dtype=jnp.int32)[None, None, :]
    ) & causal[:, :, None]
    return (causal, onehot.astype(jnp.float32))


def on_device(
    token_values,
    gate_values,
    state_in,
    state_out,
    step_size,
    log_decay,
    level_weight,
    skip_weight,
    norm_gain,
    out_weight,
):
    rows = token_values.shape[0]
    heads = step_size.shape[1]
    blocks_here = rows // STRETCH
    local_bits = blocks_here.bit_length() - 1
    seq_bits = lax.axis_size("seq").bit_length() - 1
    causal, onehot = stretch_levels()
    values = token_values.astype(jnp.float32).reshape(blocks_here, STRETCH, heads, P_SIZE)
    inputs = values * step_size.reshape(blocks_here, STRETCH, heads)[:, :, :, None]
    within = jnp.cumsum(log_decay.reshape(blocks_here, STRETCH, heads), axis=1)
    totals = within[:, -1]
    weights = level_weight.astype(jnp.float32).reshape(blocks_here, STRETCH, heads, -1)
    query_narrow = state_out.reshape(blocks_here, STRETCH, N)
    key_narrow = state_in.reshape(blocks_here, STRETCH, N)
    scores = jnp.einsum(
        "ctn,csn->cts", query_narrow, key_narrow, preferred_element_type=jnp.float32
    )
    within_heads = jnp.transpose(within, (0, 2, 1))
    gaps = jnp.where(
        causal[None, None], within_heads[:, :, :, None] - within_heads[:, :, None, :], -jnp.inf
    )
    mixing = (
        jnp.einsum("cthl,tsl->chts", weights[:, :, :, : STRETCH_BITS + 1], onehot)
        * jnp.exp(gaps)
        * scores[:, None]
    )
    output = jnp.einsum("chts,cshp->cthp", mixing, inputs, precision=HIGH)
    to_end = jnp.exp(totals[:, None, :] - within)
    key_rows = state_in.astype(jnp.float32).reshape(blocks_here, STRETCH, N)
    query_rows = state_out.astype(jnp.float32).reshape(blocks_here, STRETCH, N)
    states = jnp.einsum("csn,cshp->chnp", key_rows, inputs * to_end[:, :, :, None], precision=HIGH)
    lift = jnp.exp(within)
    block_ids = jnp.arange(blocks_here, dtype=jnp.int32)
    blocks = states
    block_totals = totals
    for depth in range(1, local_bits + 1):
        size = 2 ** (depth - 1)
        grouped = totals.reshape(blocks_here // size, size, heads)
        before = (jnp.cumsum(grouped, axis=1) - grouped).reshape(blocks_here, heads)
        upper = (block_ids >> depth - 1 & 1).astype(jnp.float32)
        sibling = jnp.bitwise_xor(block_ids >> depth - 1, 1)
        carried = blocks[sibling] * (upper[:, None] * jnp.exp(before))[:, :, None, None]
        reached = jnp.einsum("ctn,chnp->cthp", query_rows, carried, precision=HIGH)
        output = (
            output + weights[:, :, :, STRETCH_BITS + depth, None] * lift[:, :, :, None] * reached
        )
        paired = blocks.reshape(-1, 2, heads, N, P_SIZE)
        pair_totals = block_totals.reshape(-1, 2, heads)
        blocks = jnp.exp(pair_totals[:, 1])[:, :, None, None] * paired[:, 0] + paired[:, 1]
        block_totals = pair_totals[:, 0] + pair_totals[:, 1]
    ahead = jnp.cumsum(totals, axis=0) - totals
    device_state = blocks[0]
    device_total = block_totals[0]
    element_index = lax.axis_index("seq")
    spanned = jnp.zeros((heads,), jnp.float32)
    level_states = []
    for depth in range(seq_bits):
        partner, partner_total = partner_2((device_state, device_total), "seq", depth)
        upper = (element_index >> depth & 1).astype(jnp.float32)
        level_states.append(upper * jnp.exp(spanned)[:, None, None] * partner)
        device_state = jnp.where(
            upper > 0,
            jnp.exp(device_total)[:, None, None] * partner + device_state,
            jnp.exp(partner_total)[:, None, None] * device_state + partner,
        )
        spanned = spanned + upper * partner_total
        device_total = device_total + partner_total
    remote_states = jnp.stack(level_states)
    remote = jnp.einsum("ctn,mhnp->cthmp", query_rows, remote_states, precision=HIGH)
    remote_lift = jnp.exp(within + ahead[:, None, :])
    far_weights = weights[:, :, :, STRETCH_BITS + local_bits + 1 :]
    output = output + remote_lift[:, :, :, None] * jnp.einsum(
        "cthmp,cthm->cthp", remote, far_weights
    )
    mixed = (output + skip_weight[:, None] * values).reshape(rows, heads * P_SIZE)
    gated = mixed * jax.nn.silu(gate_values.astype(jnp.float32))
    square = lax.psum(jnp.sum(gated * gated, axis=1), "head")
    features = (gated * lax.rsqrt(square / (H * P_SIZE) + EPSILON)[:, None] * norm_gain).astype(
        jnp.bfloat16
    )
    product = jnp.dot(features, out_weight, preferred_element_type=jnp.float32)
    rounded = lax.optimization_barrier(product.astype(jnp.bfloat16))
    return lax.psum_scatter(
        rounded.astype(jnp.float32).astype(jnp.bfloat16), "head", scatter_dimension=0, tiled=True
    )


def solution(mesh):
    placed = (
        P("seq", "head"),
        P("seq", "head"),
        P("seq", None),
        P("seq", None),
        P("seq", "head"),
        P("seq", "head"),
        P("seq", "head", None),
        P("head"),
        P("head"),
        P("head", None),
    )
    return jax.shard_map(
        on_device, mesh=mesh, in_specs=placed, out_specs=P(("seq", "head"), None), check_vma=False
    )
```

profile of v0, /device:TPU:25, one launch (start us, length us, event | category | flops | bytes accessed | tf_op | source)
XLA Modules:
  0.0 151.3 jit_solution(8783487376070312222)
XLA Ops:
  8.7 1.2 collective-permute-start.1
  10.9 2.4 %copy.55 = f32[256,1280]{0,1:T(8,128)} copy(bf16[256,1280]{1,0:T(8,128)(2,1)} %param.10) | data formatting | bytes 1966080 | tf_op jit(solution)/shard_map/reshape | solution.py:60
  13.4 2.3 %reshape.304 = f32[4,64,20,64]{1,0,3,2:T(4,128)S(1)} reshape(f32[256,1280]{0,1:T(8,128)} %copy.55) | data formatting | bytes 2621440 | tf_op jit(solution)/shard_map/reshape | solution.py:60
  15.7 2.4 %broadcast_multiply_fusion = (f32[4,64,20,64]{1,0,3,2:T(4,128)S(1)}, f32[4,64,20,64]{1,0,3,2:T(4,128)}) fusion(f32[4,64,20]{1,0,2:T(4,128)S(1)} %copy.66, f32[4,64,20,64]{1,0,3,2:T(4,128)S(1)} %reshape.304, f32[4,64,20]{1,0,2:T(4,128)S(1)} %mul.242), kind=kLoop, calls=%fused_computation.43 | loop fusion | flops 655360 | bytes 3973120 | tf_op jit(solution)/shard_map/mul | solution.py:83
  18.1 1.4 fusion.6
  19.7 1.1 copy-done.5
  20.8 1.0 fusion.27
  27.7 1.4 copy.64
  29.0 1.3 bitcast_add_fusion.1
  30.6 1.3 reshape.300
  32.9 1.6 %copy.89 = bf16[4,64,20,7]{2,3,0,1:T(8,128)(2,1)} copy(bf16[4,64,20,7]{1,0,2,3:T(4,128)(2,1)S(1)} %slice-done) | data formatting | bytes 143360
  35.4 3.6 %gather_fusion.1 = f32[4,20,128,64]{2,3,1,0:T(8,128)} fusion(f32[2,20,128,64]{2,3,1,0:T(8,128)} %bitcast_add_fusion.1, s32[1024]{0:T(1024)S(1)} %pad_clamp_fusion), kind=kCustom, calls=%fused_computation.1 | custom fusion | bytes 5242896 | tf_op jit(solution)/shard_map/gather | solution.py:94
  39.7 2.6 %multiply_bitcast_fusion.2 = (f32[1,20,128,64]{2,3,1,0:T(8,128)}, f32[20,128,64]{1,2,0:T(8,128)S(1)}) fusion(f32[20,128,64]{1,2,0:T(8,128)} %collective-permute-done, f32[]{:T(128)S(6)} %convert_element_type.89, f32[20]{0:T(128)S(1)} %get-tuple-element.26, f32[20]{0:T(128)S(1)} %copy-done.24, pred[]{:T(512)S(6)} %gt.6, f32[1,2,20,128,64]{3,4,2,1,0:T(8,128)} %copy-done.5, ...), kind=kLoop, calls=%fused_computation.56 | loop fusion | flops 1310720 | bytes 3277045 | tf_op jit(solution)/shard_map/stack | solution.py:120
  42.3 1.3 collective-permute-start.2
  43.6 2.7 %fusion.1 = f32[4,20,64,64]{3,1,0,2:T(8,128)} fusion(bf16[4,64,20,7]{2,3,0,1:T(8,128)(2,1)S(1)} %copy-done.11, f32[4,64,64]{2,0,1:T(4,128)S(1)} %copy.61, f32[4,20,64]{2,1,0:T(8,128)S(1)} %copy-done.18, f32[4,20,64]{1,0,2:T(4,128)S(1)} %copy-done.17, pred[64,64]{1,0:T(8,128)(4,1)S(1)} %copy-done.19, pred[64,64,7,1]{1,0,2,3:T(32,128)(4,1)S(1)} %fusion.33), kind=kOutput, calls=%fused_computation.6 | convolution fusion | flops 5898240 | bytes 1521664 | tf_op jit(solution)/shard_map/cthl,tsl->chts/dot_general | solution.py:75
  46.3 3.0 %fusion.11 = f32[4,20,64,64]{3,2,1,0:T(8,128)} fusion(bf16[4,64,128,1]{2,1,3,0:T(8,128)(2,1)S(1)} %bitcast.128, f32[4,20,128,64]{2,3,1,0:T(8,128)S(1)} %copy-done.4, f32[4,20]{1,0:T(4,128)S(1)} %exponential_multiply_fusion), kind=kOutput, calls=%fused_computation.20 | convolution fusion | flops 503971840 | bytes 3998016 | tf_op jit(solution)/shard_map/ctn,chnp->cthp/dot_general | solution.py:95
  49.3 7.7 %collective-permute-done.2 = f32[20,128,64]{1,2,0:T(8,128)S(1)} collective-permute-done((f32[20,128,64]{1,2,0:T(8,128)S(1)}, f32[20,128,64]{1,2,0:T(8,128)S(1)}, u32[]{:S(2)}, u32[]{:S(2)}) %collective-permute-start.2) | collective-permute-done | bytes 655392 | tf_op jit(solution)/shard_map/ppermute | solution.py:20
  57.0 1.3 multiply_bitcast_fusion.1
  58.6 1.3 copy.74
  59.9 1.6 %copy.65 = f32[4,64,20]{1,2,0:T(8,128)} copy(f32[4,64,20]{2,1,0:T(8,128)} %get-tuple-element.11) | data formatting | bytes 40960 | tf_op jit(solution)/shard_map/mul | solution.py:97
  62.3 2.3 %gather_fusion = f32[4,20,128,64]{2,3,1,0:T(8,128)} fusion(f32[4,20,128,64]{2,3,1,0:T(8,128)S(1)} %bitcast.133, s32[1024]{0:T(1024)S(1)} %pad_clamp_fusion.1), kind=kCustom, calls=%fused_computation | custom fusion | bytes 5242896 | tf_op jit(solution)/shard_map/gather | solution.py:94
  65.4 8.6 %fusion.8 = f32[4,20,64,64]{3,2,1,0:T(8,128)S(1)} fusion(f32[4,20,64,64]{3,1,0,2:T(8,128)} %fusion.1, f32[4,64,20,64]{1,0,3,2:T(4,128)} %get-tuple-element.10), kind=kOutput, calls=%fused_computation.17 | convolution fusion | flops 251658240 | bytes 3932160 | tf_op jit(solution)/shard_map/chts,cshp->cthp/dot_general | solution.py:79
  74.0 15.1 %collective-permute-done.4 = f32[20,128,64]{1,2,0:T(8,128)} collective-permute-done((f32[20,128,64]{1,2,0:T(8,128)}, f32[20,128,64]{1,2,0:T(8,128)}, u32[]{:S(2)}, u32[]{:S(2)}) %collective-permute-start.4) | collective-permute-done | bytes 655392 | tf_op jit(solution)/shard_map/ppermute | solution.py:20
  89.1 1.2 multiply_bitcast_fusion
  90.4 4.5 %fusion = f32[4,64,20,64]{1,3,0,2:T(8,128)S(1)} fusion(f32[4,64,20,3]{1,0,2,3:T(4,128)S(1)} %slice_convert_fusion, bf16[4,64,128,1,1]{2,1,0,4,3:T(8,128)(2,1)S(1)} %bitcast.130, f32[1,20,128,64]{2,3,1,0:T(8,128)S(1)} %multiply_bitcast_fusion, f32[1,20,128,64]{2,3,1,0:T(8,128)S(1)} %copy-done.9, f32[1,20,128,64]{2,3,1,0:T(8,128)S(1)} %copy-done.8), kind=kOutput, calls=%fused_computation.3 | convolution fusion | flops 1512570880 | bytes 3403776 | tf_op jit(solution)/shard_map/ctn,mhnp->cthmp/dot_general | solution.py:121
  94.9 2.5 %fusion.4 = f32[4,64,20,64]{1,3,2,0:T(8,128)S(1)} fusion(f32[4,20,64,64]{3,2,1,0:T(8,128)S(1)} %copy-done.6, f32[4,20,64,64]{3,2,1,0:T(8,128)S(1)} %fusion.8, f32[4,64,20,64]{1,3,0,2:T(8,128)S(1)} %fusion, f32[4,64,20,64]{1,0,3,2:T(4,128)S(1)} %copy-done.2, bf16[4,64,128,1]{2,1,3,0:T(8,128)(2,1)S(1)} %bitcast.127, f32[4,20,128,64]{2,3,1,0:T(8,128)S(1)} %copy-done.3, ...), kind=kOutput, calls=%fused_computation.10 | convolution fusion | flops 506593280 | bytes 9302416 | tf_op jit(solution)/shard_map/ctn,chnp->cthp/dot_general | solution.py:95
  97.4 1.9 %copy.73 = f32[4,64,20,64]{1,0,3,2:T(4,128)S(1)} copy(f32[4,64,20,64]{1,3,2,0:T(8,128)S(1)} %fusion.4) | data formatting | bytes 2621440 | tf_op jit(solution)/shard_map/add | solution.py:127
  99.4 2.5 %reshape.302 = f32[256,1280]{0,1:T(8,128)} reshape(f32[4,64,20,64]{1,0,3,2:T(4,128)S(1)} %copy.73) | data formatting | bytes 2621440 | tf_op jit(solution)/shard_map/reshape | solution.py:127
  101.9 1.8 %multiply_reduce_fusion = f32[256]{0:T(256)S(1)} fusion(f32[256,1280]{0,1:T(8,128)} %reshape.302, bf16[256,1280]{0,1:T(8,128)(2,1)S(1)} %copy.74), kind=kLoop, calls=%fused_computation.40 | loop fusion | flops 2621184 | bytes 1967104 | tf_op jit(solution)/shard_map/reduce_sum | solution.py:129
  103.7 6.6 %psum.7 = f32[256]{0:T(256)S(1)} all-reduce(f32[256]{0:T(256)S(1)} %multiply_reduce_fusion), channel_id=1, replica_groups=mesh['seq'=8,'head'=4] {'head'}, use_global_device_ids=true, to_apply=%region_4.5 | all-reduce | flops 256 | bytes 2048 | tf_op jit(solution)/shard_map/psum | solution.py:129
  110.3 6.4 %convolution_convert_fusion = bf16[256,2560]{1,0:T(8,128)(2,1)} fusion(bf16[1280,2560]{1,0:T(8,128)(2,1)} %param.19, f32[1280]{0:T(1024)S(1)} %copy-done.30, f32[256]{0:T(256)S(1)} %add_rsqrt_fusion, f32[256,1280]{0,1:T(8,128)} %reshape.302, bf16[256,1280]{0,1:T(8,128)(2,1)S(1)} %copy.74), kind=kOutput, calls=%fused_computation.4 | convolution fusion | flops 1681326080 | bytes 9836544 | tf_op jit(solution)/shard_map/dot_general | solution.py:133
  116.6 27.9 %reduce-scatter.2.cloned.1.call-done = bf16[64,2560]{1,0:T(8,128)(2,1)} async-done(((bf16[256,2560]{1,0:T(8,128)(2,1)}), bf16[64,2560]{1,0:T(8,128)(2,1)}) %reduce-scatter.2.cloned.1.call-update) | async-done | bytes 327696 | tf_op jit(solution)/shard_map/reduce_scatter | solution.py:135
  (106 shorter events, 13.9 us)
Async XLA Ops:
  6.5 23.8 %copy-start = (bf16[256,128]{1,0:T(8,128)(2,1)S(1)}, bf16[256,128]{1,0:T(8,128)(2,1)}, u32[]{:S(2)}) copy-start(bf16[256,128]{1,0:T(8,128)(2,1)} %param.13) | copy-start | bytes 196612
  6.5 138.0 %reduce-scatter.2.cloned.1.call-start = ((), (), s32[]{:S(2)}) async-start(), calls=%async_computation.1 | async-start | bytes 1638400 | tf_op jit(solution)/shard_map/reduce_scatter | solution.py:135
  8.7 25.8 %collective-permute-start.1 = (f32[20]{0:T(128)}, f32[20]{0:T(128)}, u32[]{:S(2)}, u32[]{:S(2)}) collective-permute-start(f32[20]{0:T(128)} %get-tuple-element.8), channel_id=1, source_target_pairs={{0,4},{4,0},{8,12},{12,8},{16,20},{20,16},{24,28},{28,24},{1,5},{5... | collective-permute-start | bytes 248 | tf_op jit(solution)/shard_map/ppermute | solution.py:20
  10.0 9.8 %copy-start.22 = (f32[20]{0:T(128)}, f32[20]{0:T(128)S(1)}, u32[]{:S(2)}) copy-start(f32[20]{0:T(128)S(1)} %exponential_bitcast_fusion) | copy-start | bytes 244
  19.5 8.0 %copy-start.15 = (bf16[256,20,12]{0,1,2:T(8,128)(2,1)S(1)}, bf16[256,20,12]{0,1,2:T(8,128)(2,1)}, u32[]{:S(2)}) copy-start(bf16[256,20,12]{0,1,2:T(8,128)(2,1)} %param.16) | copy-start | bytes 368644
  21.8 17.9 %collective-permute-start = (f32[20,128,64]{1,2,0:T(8,128)}, f32[20,128,64]{1,2,0:T(8,128)}, u32[]{:S(2)}, u32[]{:S(2)}) collective-permute-start(f32[20,128,64]{1,2,0:T(8,128)} %fusion.27), channel_id=1, source_target_pairs={{0,4},{4,0},{8,12},{12,8},{16,20},{20,16},{24,28},{28,24},{1,5},{5... | collective-permute-start | bytes 1966088 | tf_op jit(solution)/shard_map/ppermute | solution.py:20
  27.6 2.6 %copy-start.7 = (bf16[4,64,20,12]{1,0,2,3:T(4,128)(2,1)}, bf16[4,64,20,12]{1,0,2,3:T(4,128)(2,1)S(1)}, u32[]{:S(2)}) copy-start(bf16[4,64,20,12]{1,0,2,3:T(4,128)(2,1)S(1)} %reshape.296) | copy-start | bytes 368644
  27.7 2.7 %copy-start.28 = (s32[4]{0:T(128)S(1)}, s32[4]{0:T(128)}, u32[]{:S(2)}) copy-start(s32[4]{0:T(128)} %fusion.43) | copy-start | bytes 52
  30.3 2.5 %copy-start.20 = (f32[4,1,20]{2,1,0:T(1,128)S(1)}, f32[4,1,20]{2,1,0:T(1,128)}, u32[]{:S(2)}) copy-start(f32[4,1,20]{2,1,0:T(1,128)} %get-tuple-element.17) | copy-start | bytes 964
  30.3 2.5 %copy-start.21 = (f32[2,2,20]{2,1,0:T(2,128)S(1)}, f32[2,2,20]{2,1,0:T(2,128)}, u32[]{:S(2)}) copy-start(f32[2,2,20]{2,1,0:T(2,128)} %reduce_window_sum.42) | copy-start | bytes 964
  30.3 2.5 %copy-start.27 = (f32[4]{0:T(128)S(1)}, f32[4]{0:T(128)}, u32[]{:S(2)}) copy-start(f32[4]{0:T(128)} %and_convert_fusion.1) | copy-start | bytes 52
  30.3 2.6 %slice-start = ((bf16[4,64,20,12]{1,0,2,3:T(4,128)(2,1)}), bf16[4,64,20,7]{1,0,2,3:T(4,128)(2,1)S(1)}, s32[]{:S(2)}) async-start(bf16[4,64,20,12]{1,0,2,3:T(4,128)(2,1)} %copy-done.7), calls=%async_computation.2 | async-start | bytes 286720 | tf_op jit(solution)/shard_map/slice | solution.py:75
  35.1 4.5 %copy-start.23 = (f32[20]{0:T(128)S(1)}, f32[20]{0:T(128)}, u32[]{:S(2)}) copy-start(f32[20]{0:T(128)} %copy-done.22) | copy-start | bytes 244
  35.1 4.5 %copy-start.24 = (f32[20]{0:T(128)S(1)}, f32[20]{0:T(128)}, u32[]{:S(2)}) copy-start(f32[20]{0:T(128)} %get-tuple-element.7) | copy-start | bytes 244
  35.1 3.8 %collective-permute-start.3 = (f32[20]{0:T(128)S(1)}, f32[20]{0:T(128)S(1)}, u32[]{:S(2)}, u32[]{:S(2)}) collective-permute-start(f32[20]{0:T(128)S(1)} %get-tuple-element.6), channel_id=1, source_target_pairs={{0,8},{4,12},{8,0},{12,4},{16,24},{20,28},{24,16},{28,20},{1,9},{5... | collective-permute-start | bytes 248 | tf_op jit(solution)/shard_map/ppermute | solution.py:20
  39.0 4.6 %copy-start.11 = (bf16[4,64,20,7]{2,3,0,1:T(8,128)(2,1)S(1)}, bf16[4,64,20,7]{2,3,0,1:T(8,128)(2,1)}, u32[]{:S(2)}) copy-start(bf16[4,64,20,7]{2,3,0,1:T(8,128)(2,1)} %copy.89) | copy-start | bytes 215044
  39.0 4.6 %copy-start.17 = (f32[4,20,64]{1,0,2:T(4,128)S(1)}, f32[4,20,64]{1,0,2:T(4,128)}, u32[]{:S(2)}) copy-start(f32[4,20,64]{1,0,2:T(4,128)} %copy.59) | copy-start | bytes 61444
  39.0 4.6 %copy-start.18 = (f32[4,20,64]{2,1,0:T(8,128)S(1)}, f32[4,20,64]{2,1,0:T(8,128)}, u32[]{:S(2)}) copy-start(f32[4,20,64]{2,1,0:T(8,128)} %copy.60) | copy-start | bytes 61444
  42.3 4.0 %copy-start.4 = (f32[4,20,128,64]{2,3,1,0:T(8,128)S(1)}, f32[4,20,128,64]{2,3,1,0:T(8,128)}, u32[]{:S(2)}) copy-start(f32[4,20,128,64]{2,3,1,0:T(8,128)} %gather_fusion.1) | copy-start | bytes 7864324
  42.3 14.7 %collective-permute-start.2 = (f32[20,128,64]{1,2,0:T(8,128)S(1)}, f32[20,128,64]{1,2,0:T(8,128)S(1)}, u32[]{:S(2)}, u32[]{:S(2)}) collective-permute-start(f32[20,128,64]{1,2,0:T(8,128)S(1)} %get-tuple-element.14), channel_id=1, source_target_pairs={{0,8},{4,12},{8,0},{12,4},{16,24},{20,28},{24,16},{28,20},{1,9},{5... | collective-permute-start | bytes 1966088 | tf_op jit(solution)/shard_map/ppermute | solution.py:20
  49.3 9.2 %copy-start.26 = (s32[4]{0:T(128)S(1)}, s32[4]{0:T(128)}, u32[]{:S(2)}) copy-start(s32[4]{0:T(128)} %fusion.42) | copy-start | bytes 52
  49.3 12.2 %copy-start.10 = (f32[4,64,20]{2,1,0:T(8,128)S(1)}, f32[4,64,20]{2,1,0:T(8,128)}, u32[]{:S(2)}) copy-start(f32[4,64,20]{2,1,0:T(8,128)} %get-tuple-element.12) | copy-start | bytes 61444
  58.3 30.8 %collective-permute-start.4 = (f32[20,128,64]{1,2,0:T(8,128)}, f32[20,128,64]{1,2,0:T(8,128)}, u32[]{:S(2)}, u32[]{:S(2)}) collective-permute-start(f32[20,128,64]{1,2,0:T(8,128)} %get-tuple-element.16), channel_id=1, source_target_pairs={{0,16},{4,20},{8,24},{12,28},{16,0},{20,4},{24,8},{28,12},{1,17},{... | collective-permute-start | bytes 1966088 | tf_op jit(solution)/shard_map/ppermute | solution.py:20
  65.4 24.9 %copy-start.8 = (f32[1,20,128,64]{2,3,1,0:T(8,128)S(1)}, f32[1,20,128,64]{2,3,1,0:T(8,128)}, u32[]{:S(2)}) copy-start(f32[1,20,128,64]{2,3,1,0:T(8,128)} %get-tuple-element.13) | copy-start | bytes 1966084
  65.4 24.9 %copy-start.9 = (f32[1,20,128,64]{2,3,1,0:T(8,128)S(1)}, f32[1,20,128,64]{2,3,1,0:T(8,128)}, u32[]{:S(2)}) copy-start(f32[1,20,128,64]{2,3,1,0:T(8,128)} %get-tuple-element.15) | copy-start | bytes 1966084
  65.4 29.5 %copy-start.6 = (f32[4,20,64,64]{3,2,1,0:T(8,128)S(1)}, f32[4,20,64,64]{3,2,1,0:T(8,128)}, u32[]{:S(2)}) copy-start(f32[4,20,64,64]{3,2,1,0:T(8,128)} %fusion.11) | copy-start | bytes 3932164
  90.3 4.6 %copy-start.2 = (f32[4,64,20,64]{1,0,3,2:T(4,128)S(1)}, f32[4,64,20,64]{1,0,3,2:T(4,128)}, u32[]{:S(2)}) copy-start(f32[4,64,20,64]{1,0,3,2:T(4,128)} %copy-done.1) | copy-start | bytes 3932164
  90.3 4.6 %copy-start.3 = (f32[4,20,128,64]{2,3,1,0:T(8,128)S(1)}, f32[4,20,128,64]{2,3,1,0:T(8,128)}, u32[]{:S(2)}) copy-start(f32[4,20,128,64]{2,3,1,0:T(8,128)} %gather_fusion) | copy-start | bytes 7864324
  90.3 4.6 %copy-start.13 = (f32[4,64,20]{1,2,0:T(8,128)S(1)}, f32[4,64,20]{1,2,0:T(8,128)}, u32[]{:S(2)}) copy-start(f32[4,64,20]{1,2,0:T(8,128)} %copy.65) | copy-start | bytes 61444
  90.4 4.6 %copy-start.14 = (f32[4,64,20]{1,2,0:T(8,128)S(1)}, f32[4,64,20]{1,2,0:T(8,128)}, u32[]{:S(2)}) copy-start(f32[4,64,20]{1,2,0:T(8,128)} %copy.68) | copy-start | bytes 61444
  90.4 4.6 %copy-start.25 = (f32[20]{0:T(128)S(1)}, f32[20]{0:T(128)}, u32[]{:S(2)}) copy-start(f32[20]{0:T(128)} %param.17) | copy-start | bytes 244
  99.4 10.9 %copy-start.30 = (f32[1280]{0:T(1024)S(1)}, f32[1280]{0:T(1024)}, u32[]{:S(2)}) copy-start(f32[1280]{0:T(1024)} %param.18) | copy-start | bytes 15364
  (6 other events, 13.2 us)
Sparse Core Ops, SparseCore 0:
  116.8 27.6 reduce-scatter.1
where the time goes:
time: 154 us; the launch traced here: 151 us
  waiting for transfers between devices  50.6 us (33%)
  matrix products  29.1 us (19%)
  local copies, waits for them, and re-layouts  26.5 us (17%)
  other arithmetic  21.4 us (14%)
  between operations  13.9 us (9%)
  blocking collectives  6.59 us (4%)
  starting transfers between devices  3.18 us (2%)
    reduce_scatter x1, waiting for transfers between devices, on_device(): lax.psum_scatter(rounded.astype(jnp.float32).astype(jnp.bfloat16), 'head'...  27.9 us
    ppermute x5, waiting for transfers between devices, partner_2(): return lax.ppermute(value, axis, pairs)  22.8 us
    dot_general x1, matrix products, on_device(): output = jnp.einsum('chts,cshp->cthp', mixing, inputs, precision=HIGH)  8.57 us
    psum x1, blocking collectives, on_device(): square = lax.psum(jnp.sum(gated * gated, axis=1), 'head')  6.59 us
    dot_general x1, matrix products, on_device(): product = jnp.dot(features, out_weight, preferred_element_type=jnp.float32)  6.35 us
    gather x2, local copies, waits for them, and re-layouts, on_device(): blocks[sibling] * (upper[:, None] * jnp.exp(before))[:, :, None, None]  5.89 us
    dot_general x2, matrix products, on_device(): reached = jnp.einsum('ctn,chnp->cthp', query_rows, carried, precision=HIGH)  5.45 us
    another operation x3, other arithmetic, on_device(): remote_states = jnp.stack(level_states)  5.07 us
  transfers between devices with their start and end apart: 6, of which 3 were waited for; matrix products, arithmetic and copies ran while one was open for 32% of the time, Pallas kernels for 0%

commit v1 on v0

v1 whole, which is shorter than its diff:
```python
import functools

import jax
import jax.numpy as jnp
from jax import lax
from jax.experimental import pallas as pl
from jax.experimental.pallas import tpu as pltpu
from jax.sharding import PartitionSpec as P

P_SIZE = 64
EPSILON = 1e-05
HIGH = lax.Precision.HIGHEST
MESH = pl.DeviceIdType.MESH
LANES = 128
F32 = jnp.float32
BF16 = jnp.bfloat16


def dot(a, b, precision=None):
    return jnp.dot(a, b, preferred_element_type=F32, precision=precision)


def dot_nt(a, b):
    return lax.dot_general(a, b, (((1,), (1,)), ((), ())), preferred_element_type=F32)


def partner_of(axis, depth):
    me = lax.axis_index(axis)
    bit = (me // 2**depth) % 2
    return bit, me + (1 - 2 * bit) * 2**depth


def mixer_kernel(
    seq_bits,
    width_all,
    col,
    GROUP,
    head_devices,
    tv_ref,
    gate_ref,
    key_ref,
    query_ref,
    step_ref,
    decay_ref,
    weight_ref,
    skip_ref,
    gain_ref,
    w_hbm,
    out_ref,
    w_ref,
    tvt,
    xt,
    mixed,
    silu_t,
    gain_t,
    feat,
    lw,
    cum_r,
    cum_c,
    lift,
    score_t,
    level_of,
    own,
    got,
    e_own,
    e_got,
    factor,
    square,
    sq_send,
    sq_got,
    core_send,
    core_got,
    far_send,
    far_got,
    w_sem,
    state_ss,
    state_rs,
    e_ss,
    e_rs,
    sq_ss,
    sq_rs,
    core_ss,
    core_rs,
    far_ss,
    far_rs,
):
    rows = tv_ref.shape[0]
    heads = step_ref.shape[0]
    tiles = rows // LANES
    groups = heads // GROUP
    span = GROUP * P_SIZE
    lane_bits = LANES.bit_length() - 1
    local_bits = rows.bit_length() - 1
    levels_here = local_bits + 1
    n_col = w_ref.shape[1] // col
    block = rows // head_devices
    chips = head_devices // 2

    barrier = pltpu.get_barrier_semaphore()
    seq_partner = [partner_of("seq", d) for d in range(seq_bits)]
    core_bit, core_peer = partner_of("head", 0)
    chip = lax.axis_index("head") // 2
    chip_at = [(chip + r) % chips for r in range(chips)]
    far_peer = [2 * at + core_bit for at in chip_at]
    for _, peer in seq_partner:
        pl.semaphore_signal(barrier, inc=1, device_id={"seq": peer}, device_id_type=MESH)
    for peer in [core_peer] + far_peer[1:]:
        pl.semaphore_signal(barrier, inc=1, device_id={"head": peer}, device_id_type=MESH)

    w_copy = pltpu.make_async_copy(w_hbm, w_ref, w_sem)
    w_copy.start()

    def send(axis, peer, src, dst, ss, rs):
        return pltpu.make_async_remote_copy(
            src_ref=src,
            dst_ref=dst,
            send_sem=ss,
            recv_sem=rs,
            device_id={axis: peer},
            device_id_type=MESH,
        )

    def state_copy(d, g):
        return send(
            "seq", seq_partner[d][1], own.at[d, g], got.at[d, g], state_ss.at[d, g], state_rs.at[d, g]
        )

    def total_copy(d):
        return send("seq", seq_partner[d][1], e_own.at[d], e_got.at[d], e_ss.at[d], e_rs.at[d])

    u_at = lax.broadcasted_iota(jnp.int32, (rows, rows), 0)
    t_at = lax.broadcasted_iota(jnp.int32, (rows, rows), 1)
    decay = decay_ref[...]
    cum = dot(decay, (u_at <= t_at).astype(F32), HIGH)
    to_end = jnp.exp(dot(decay, (u_at > t_at).astype(F32), HIGH))
    total = dot(decay, jnp.ones((rows, LANES), F32), HIGH)
    cum_r[...] = cum
    steps = step_ref[...]
    key_scale = steps * to_end
    e_own[0] = jnp.exp(total)

    for j in range(tv_ref.shape[1] // LANES):
        tvt[pl.ds(j * LANES, LANES), :] = jnp.transpose(
            tv_ref[:, pl.ds(j * LANES, LANES)].astype(F32)
        )

    pl.semaphore_wait(barrier, seq_bits + chips)
    total_copy(0).start()
    keys = key_ref[...]
    for g in range(groups):
        parts = []
        for h in range(g * GROUP, (g + 1) * GROUP):
            value = tvt[pl.ds(h * P_SIZE, P_SIZE), :]
            parts.append((value * key_scale[h : h + 1, :]).astype(BF16))
            xt[pl.ds(h * P_SIZE, P_SIZE), :] = (value * steps[h : h + 1, :]).astype(BF16)
        own[0, g] = dot(jnp.concatenate(parts, axis=0), keys).astype(BF16)
        state_copy(0, g).start()

    lift[...] = jnp.exp(cum)
    cum_c[...] = jnp.transpose(cum)
    for l in range(weight_ref.shape[0]):
        lw[l] = weight_ref[l].astype(F32)
    queries = query_ref[...]
    s_full = dot_nt(keys, queries)
    score_t[...] = jnp.where(u_at <= t_at, s_full, 0.0)
    apart = jnp.bitwise_xor(u_at[:LANES, :LANES], t_at[:LANES, :LANES])
    level = jnp.zeros((LANES, LANES), jnp.int32)
    for shift in range(lane_bits):
        level = level + (apart >= 1 << shift).astype(jnp.int32)
    level_of[...] = level
    square[...] = jnp.zeros_like(square)
    for j in range(gate_ref.shape[1] // LANES):
        gain_t[pl.ds(j * LANES, LANES), :] = jnp.transpose(
            jnp.broadcast_to(gain_ref[:, pl.ds(j * LANES, LANES)], (LANES, LANES))
        )

    def local_part(g):
        for h in range(g * GROUP, (g + 1) * GROUP):
            at = pl.ds(h * P_SIZE, P_SIZE)
            x = xt[at, :]
            for bt in range(tiles):
                lanes = pl.ds(bt * LANES, LANES)
                row = cum_r[pl.ds(h, 1), lanes]
                stack = []
                for bs in range(bt + 1):
                    sub = pl.ds(bs * LANES, LANES)
                    column = cum_c[sub, pl.ds(h, 1)]
                    fade = jnp.exp(jnp.minimum(row - column, 0.0)) * score_t[sub, lanes]
                    if bs == bt:
                        level_now = level_of[...]
                        weight = jnp.broadcast_to(lw[0, pl.ds(h, 1), lanes], (LANES, LANES))
                        for l in range(1, lane_bits + 1):
                            weight = jnp.where(level_now == l, lw[l, pl.ds(h, 1), lanes], weight)
                    else:
                        weight = lw[lane_bits + (bt ^ bs).bit_length(), pl.ds(h, 1), lanes]
                    stack.append((fade * weight).astype(BF16))
                mix = stack[0] if bt == 0 else jnp.concatenate(stack, axis=0)
                mixed[at, lanes] = dot(x[:, : (bt + 1) * LANES], mix) + skip_ref[h] * tvt[at, lanes]
        for j in range(g * span // LANES, (g + 1) * span // LANES):
            gate = jnp.transpose(gate_ref[:, pl.ds(j * LANES, LANES)].astype(F32))
            silu_t[pl.ds(j * LANES, LANES), :] = gate / (1.0 + jnp.exp(-gate))

    def far_part(d, g):
        bit, _ = seq_partner[d]
        up = bit.astype(F32)
        if g == 0:
            total_copy(d).wait()
            mine, theirs = e_own[d], e_got[d]
            reach = jnp.ones_like(mine) if d == 0 else factor[d]
            if d + 1 < seq_bits:
                factor[d + 1] = reach * (up * theirs + (1.0 - up))
                e_own[d + 1] = mine * theirs
                total_copy(d + 1).start()
        state_copy(d, g).wait_recv()
        if d + 1 < seq_bits:
            mine, theirs = e_own[d], e_got[d]
            keep = up + (1.0 - up) * theirs
            take = up * mine + (1.0 - up)
            for i in range(GROUP):
                h = g * GROUP + i
                at = pl.ds(i * P_SIZE, P_SIZE)
                own[d + 1, g, at, :] = (
                    own[d, g, at, :].astype(F32) * keep[h : h + 1, :]
                    + got[d, g, at, :].astype(F32) * take[h : h + 1, :]
                ).astype(BF16)
            state_copy(d + 1, g).start()
        reached = dot_nt(got[d, g], query_ref[...])
        for i in range(GROUP):
            h = g * GROUP + i
            at = pl.ds(h * P_SIZE, P_SIZE)
            scale = lw[levels_here + d, pl.ds(h, 1), :] * lift[pl.ds(h, 1), :] * up
            if d > 0:
                reach = factor[d, pl.ds(h, 1), :]
                scale = scale * jnp.concatenate([reach] * tiles, axis=1)
            mixed[at, :] += reached[i * P_SIZE : (i + 1) * P_SIZE] * scale

    def finish_group(g):
        at = pl.ds(g * span, span)
        gated = mixed[at, :] * silu_t[at, :]
        square[...] += jnp.sum((gated * gated).reshape(span // 8, 8, rows), axis=0)
        gain = jnp.concatenate([gain_t[at, :]] * tiles, axis=1)
        feat[:, at] = jnp.transpose(gated * gain).astype(BF16)

    for k in range(groups + seq_bits):
        if k < groups:
            local_part(k)
        for d in range(seq_bits):
            g = k - d
            if 0 <= g < groups:
                far_part(d, g)
                if d == seq_bits - 1:
                    finish_group(g)

    sq_send[0] = square[...]
    sq_core = send("head", core_peer, sq_send.at[0], sq_got.at[0], sq_ss.at[0], sq_rs.at[0])
    sq_core.start()
    w_copy.wait()

    def core_copy(part, j):
        return send(
            "head",
            core_peer,
            core_send.at[part, j],
            core_got.at[part, j],
            core_ss.at[part, j],
            core_rs.at[part, j],
        )

    def far_copy(r, j):
        return send(
            "head",
            far_peer[r],
            far_send.at[r - 1, j],
            far_got.at[r - 1, j],
            far_ss.at[r - 1, j],
            far_rs.at[r - 1, j],
        )

    mine_at = core_bit * block
    theirs_at = (1 - core_bit) * block

    def project(r, j):
        wide = pl.ds(j * col, col)
        at = chip_at[r] * (2 * block)
        theirs = feat[pl.ds(pl.multiple_of(at + theirs_at, block), block), :]
        mine = feat[pl.ds(pl.multiple_of(at + mine_at, block), block), :]
        product = dot(jnp.concatenate([theirs, mine], axis=0), w_ref[:, wide])
        core_send[r, j] = product[:block].astype(BF16)
        core_copy(r, j).start()
        return product[block:]

    def forward(r, j, value):
        core_copy(r, j).wait_recv()
        far_send[r - 1, j] = (value + core_got[r, j].astype(F32)).astype(BF16)
        far_copy(r, j).start()

    held = None
    for r in range(1, chips):
        for j in range(n_col):
            fresh = project(r, j)
            if held is not None:
                forward(*held)
            held = (r, j, fresh)
    sq_core.wait()
    pair_square = square[...] + sq_got[0]
    sq_send[1] = pair_square
    sq_far = [
        send(
            "head", far_peer[r], sq_send.at[1], sq_got.at[r], sq_ss.at[r], sq_rs.at[r]
        )
        for r in range(1, chips)
    ]
    for copy in sq_far:
        copy.start()
    kept = []
    for j in range(n_col):
        kept.append(project(0, j))
        if j == 0:
            forward(*held)
    for copy in sq_far:
        copy.wait()
    for r in range(1, chips):
        pair_square = pair_square + sq_got[r]
    total_square = jnp.sum(pair_square, axis=0, keepdims=True)
    norm = lax.rsqrt(total_square / width_all + EPSILON)
    columns = jnp.transpose(jnp.broadcast_to(norm, (LANES, rows)))
    gain_t[pl.ds(0, rows), :] = columns
    me = lax.axis_index("head")
    norm_mine = gain_t[pl.ds(pl.multiple_of(me * block, block), block), :]
    norm_wide = jnp.concatenate([norm_mine] * (col // LANES), axis=1)
    for j in range(n_col):
        core_copy(0, j).wait_recv()
        value = kept[j] + core_got[0, j].astype(F32)
        for r in range(1, chips):
            far_copy(r, j).wait_recv()
            value = value + far_got[r - 1, j].astype(F32)
        out_ref[:, pl.ds(j * col, col)] = (value * norm_wide).astype(BF16)

    for j in range(n_col):
        for r in range(chips):
            core_copy(r, j).wait_send()
        for r in range(1, chips):
            far_copy(r, j).wait_send()
    for d in range(seq_bits):
        for g in range(groups):
            state_copy(d, g).wait_send()


def on_device(
    token_values,
    gate_values,
    state_in,
    state_out,
    step_size,
    log_decay,
    level_weight,
    skip_weight,
    norm_gain,
    out_weight,
):
    rows, width = token_values.shape
    heads = step_size.shape[1]
    n_state = state_in.shape[1]
    levels = level_weight.shape[2]
    model = out_weight.shape[1]
    seq_bits = lax.axis_size("seq").bit_length() - 1
    head_devices = lax.axis_size("head")
    group = 4 if heads % 4 == 0 else 2
    groups = heads // group
    span = group * P_SIZE
    chips = head_devices // 2
    col = 512
    n_col = model // col
    block = rows // head_devices
    vmem = pl.BlockSpec(memory_space=pltpu.VMEM)
    dma = pltpu.SemaphoreType.DMA
    scratch = [
        pltpu.VMEM((width, model), BF16),
        pltpu.VMEM((width, rows), F32),
        pltpu.VMEM((width, rows), BF16),
        pltpu.VMEM((width, rows), F32),
        pltpu.VMEM((width, rows), F32),
        pltpu.VMEM((width, LANES), F32),
        pltpu.VMEM((rows, width), BF16),
        pltpu.VMEM((levels, heads, rows), F32),
        pltpu.VMEM((heads, rows), F32),
        pltpu.VMEM((rows, heads), F32),
        pltpu.VMEM((heads, rows), F32),
        pltpu.VMEM((rows, rows), F32),
        pltpu.VMEM((LANES, LANES), jnp.int32),
        pltpu.VMEM((seq_bits, groups, span, n_state), BF16),
        pltpu.VMEM((seq_bits, groups, span, n_state), BF16),
        pltpu.VMEM((seq_bits, heads, LANES), F32),
        pltpu.VMEM((seq_bits, heads, LANES), F32),
        pltpu.VMEM((seq_bits, heads, LANES), F32),
        pltpu.VMEM((8, rows), F32),
        pltpu.VMEM((2, 8, rows), F32),
        pltpu.VMEM((chips, 8, rows), F32),
        pltpu.VMEM((chips, n_col, block, col), BF16),
        pltpu.VMEM((chips, n_col, block, col), BF16),
        pltpu.VMEM((chips - 1, n_col, block, col), BF16),
        pltpu.VMEM((chips - 1, n_col, block, col), BF16),
        dma,
        dma((seq_bits, groups)),
        dma((seq_bits, groups)),
        dma((seq_bits,)),
        dma((seq_bits,)),
        dma((chips,)),
        dma((chips,)),
        dma((chips, n_col)),
        dma((chips, n_col)),
        dma((chips - 1, n_col)),
        dma((chips - 1, n_col)),
    ]
    return pl.pallas_call(
        functools.partial(
            mixer_kernel, seq_bits, float(width * head_devices), col, group, head_devices
        ),
        out_shape=jax.ShapeDtypeStruct((block, model), BF16),
        in_specs=[vmem] * 7
        + [pl.BlockSpec(memory_space=pltpu.SMEM), vmem, pl.BlockSpec(memory_space=pl.ANY)],
        out_specs=vmem,
        scratch_shapes=scratch,
        compiler_params=pltpu.CompilerParams(
            collective_id=0, has_side_effects=True, vmem_limit_bytes=48 * 1024 * 1024
        ),
        cost_estimate=pl.CostEstimate(
            flops=2 * rows * width * (model + 4 * rows), bytes_accessed=2 * width * model, transcendentals=heads * rows * rows
        ),
        name="mixer",
    )(
        token_values,
        gate_values,
        state_in,
        state_out,
        jnp.transpose(step_size),
        jnp.transpose(log_decay),
        jnp.transpose(level_weight, (2, 1, 0)),
        skip_weight,
        norm_gain.reshape(1, width),
        out_weight,
    )


def solution(mesh):
    placed = (
        P("seq", "head"),
        P("seq", "head"),
        P("seq", None),
        P("seq", None),
        P("seq", "head"),
        P("seq", "head"),
        P("seq", "head", None),
        P("head"),
        P("head"),
        P("head", None),
    )
    return jax.shard_map(
        on_device, mesh=mesh, in_specs=placed, out_specs=P(("seq", "head"), None), check_vma=False
    )
```

time: 154 us -> 48.9 us (0.32)
  the two profiles are of different devices: /device:TPU:25 before, /device:TPU:9 now
where the time goes in v1:
time: 48.9 us; the launch traced here: 48.4 us
  Pallas kernels  40 us (82%)
  local copies, waits for them, and re-layouts  8.32 us (17%)
    pallas_call x1, Pallas kernels, on_device(): pl.pallas_call(functools.partial(mixer_kernel, seq_bits, float(width * he...  40 us
    unnamed x17, local copies, waits for them, and re-layouts  7.62 us

profile of v1, /device:TPU:9, one launch (start us, length us, event | category | flops | bytes accessed | tf_op | source)
XLA Modules:
  0.0 48.4 jit_solution(11156546082904860644)
XLA Ops:
  0.0 0.7 %reshape.3.gain_ref = f32[1,1280]{1,0:T(1,128)S(1)} reshape(f32[1280]{0:T(1024)} %param.18) | data formatting | bytes 10240 | tf_op jit(solution)/shard_map/reshape | solution.py:440
  0.7 0.0 copy-start
  0.7 1.1 %copy-done = bf16[256,1280]{1,0:T(8,128)(2,1)S(1)} copy-done((bf16[256,1280]{1,0:T(8,128)(2,1)S(1)}, bf16[256,1280]{1,0:T(8,128)(2,1)}, u32[]{:S(2)}) %copy-start) | copy-done | bytes 655384
  1.8 0.0 copy-start.1
  1.8 1.1 %copy-done.1 = bf16[256,1280]{1,0:T(8,128)(2,1)S(1)} copy-done((bf16[256,1280]{1,0:T(8,128)(2,1)S(1)}, bf16[256,1280]{1,0:T(8,128)(2,1)}, u32[]{:S(2)}) %copy-start.1) | copy-done | bytes 655384
  2.9 0.0 copy-start.2
  2.9 0.9 %copy-done.2 = bf16[256,20,12]{0,1,2:T(8,128)(2,1)S(1)} copy-done((bf16[256,20,12]{0,1,2:T(8,128)(2,1)S(1)}, bf16[256,20,12]{0,1,2:T(8,128)(2,1)}, u32[]{:S(2)}) %copy-start.2) | copy-done | bytes 122904
  3.8 0.0 copy-start.3
  3.8 0.8 %copy-done.3 = bf16[256,128]{1,0:T(8,128)(2,1)S(1)} copy-done((bf16[256,128]{1,0:T(8,128)(2,1)S(1)}, bf16[256,128]{1,0:T(8,128)(2,1)}, u32[]{:S(2)}) %copy-start.3) | copy-done | bytes 65560
  4.6 0.0 copy-start.4
  4.6 0.8 %copy-done.4 = bf16[256,128]{1,0:T(8,128)(2,1)S(1)} copy-done((bf16[256,128]{1,0:T(8,128)(2,1)S(1)}, bf16[256,128]{1,0:T(8,128)(2,1)}, u32[]{:S(2)}) %copy-start.4) | copy-done | bytes 65560
  5.5 0.0 copy-start.5
  5.5 0.7 %copy-done.5 = f32[256,20]{0,1:T(8,128)S(1)} copy-done((f32[256,20]{0,1:T(8,128)S(1)}, f32[256,20]{0,1:T(8,128)}, u32[]{:S(2)}) %copy-start.5) | copy-done | bytes 20504
  6.2 0.0 copy-start.6
  6.2 0.7 %copy-done.6 = f32[256,20]{0,1:T(8,128)S(1)} copy-done((f32[256,20]{0,1:T(8,128)S(1)}, f32[256,20]{0,1:T(8,128)}, u32[]{:S(2)}) %copy-start.6) | copy-done | bytes 20504
  6.9 0.0 copy-start.7
  6.9 0.7 %copy-done.7 = f32[20]{0:T(128)S(1)} copy-done((f32[20]{0:T(128)S(1)}, f32[20]{0:T(128)}, u32[]{:S(2)}) %copy-start.7) | copy-done | bytes 104
  7.6 40.0 %mixer.1 = bf16[64,2560]{1,0:T(8,128)(2,1)S(1)} custom-call(bf16[256,1280]{1,0:T(8,128)(2,1)S(1)} %copy-done, bf16[256,1280]{1,0:T(8,128)(2,1)S(1)} %copy-done.1, bf16[256,128]{1,0:T(8,128)(2,1)S(1)} %copy-done.3, bf16[256,128]{1,0:T(8,128)(2,1)S(1)} %copy-done.4, f32[20,256]{1,0:T(8,128)S(1)} %bitcast.4, f32[20,256]{1,0:T(8,128)S(1)} %bitcast.5, ...), custom_call_target="tpu_custom_call" | custom-call | flops 2348810240 | bytes 6553600 | tf_op jit(solution)/shard_map/mixer/pallas_call | solution.py:415
  47.6 0.7 %copy.12 = bf16[64,2560]{1,0:T(8,128)(2,1)} copy(bf16[64,2560]{1,0:T(8,128)(2,1)S(1)} %mixer.1) | data formatting | bytes 655360
Async XLA Ops:
  0.7 1.1 %copy-start = (bf16[256,1280]{1,0:T(8,128)(2,1)S(1)}, bf16[256,1280]{1,0:T(8,128)(2,1)}, u32[]{:S(2)}) copy-start(bf16[256,1280]{1,0:T(8,128)(2,1)} %tv_ref.1) | copy-start | bytes 1966084
  1.8 1.1 %copy-start.1 = (bf16[256,1280]{1,0:T(8,128)(2,1)S(1)}, bf16[256,1280]{1,0:T(8,128)(2,1)}, u32[]{:S(2)}) copy-start(bf16[256,1280]{1,0:T(8,128)(2,1)} %gate_ref.1) | copy-start | bytes 1966084
  2.9 0.9 %copy-start.2 = (bf16[256,20,12]{0,1,2:T(8,128)(2,1)S(1)}, bf16[256,20,12]{0,1,2:T(8,128)(2,1)}, u32[]{:S(2)}) copy-start(bf16[256,20,12]{0,1,2:T(8,128)(2,1)} %param.16) | copy-start | bytes 368644
  3.8 0.8 %copy-start.3 = (bf16[256,128]{1,0:T(8,128)(2,1)S(1)}, bf16[256,128]{1,0:T(8,128)(2,1)}, u32[]{:S(2)}) copy-start(bf16[256,128]{1,0:T(8,128)(2,1)} %key_ref.1) | copy-start | bytes 196612
  4.6 0.8 %copy-start.4 = (bf16[256,128]{1,0:T(8,128)(2,1)S(1)}, bf16[256,128]{1,0:T(8,128)(2,1)}, u32[]{:S(2)}) copy-start(bf16[256,128]{1,0:T(8,128)(2,1)} %query_ref.1) | copy-start | bytes 196612
  5.5 0.7 %copy-start.5 = (f32[256,20]{0,1:T(8,128)S(1)}, f32[256,20]{0,1:T(8,128)}, u32[]{:S(2)}) copy-start(f32[256,20]{0,1:T(8,128)} %param.14) | copy-start | bytes 61444
  6.2 0.7 %copy-start.6 = (f32[256,20]{0,1:T(8,128)S(1)}, f32[256,20]{0,1:T(8,128)}, u32[]{:S(2)}) copy-start(f32[256,20]{0,1:T(8,128)} %param.15) | copy-start | bytes 61444
  6.9 0.7 %copy-start.7 = (f32[20]{0:T(128)S(1)}, f32[20]{0:T(128)}, u32[]{:S(2)}) copy-start(f32[20]{0:T(128)} %skip_ref.1) | copy-start | bytes 244

commit v2 on v1

--- a/solution.py
+++ b/solution.py
@@ -36,6 +36,17 @@
     col,
     GROUP,
     head_devices,
+    tv_hbm,
+    gate_hbm,
+    key_hbm,
+    query_hbm,
+    step_hbm,
+    decay_hbm,
+    weight_hbm,
+    skip_ref,
+    gain_hbm,
+    w_hbm,
+    out_ref,
     tv_ref,
     gate_ref,
     key_ref,
@@ -43,10 +54,7 @@
     step_ref,
     decay_ref,
     weight_ref,
-    skip_ref,
     gain_ref,
-    w_hbm,
-    out_ref,
     w_ref,
     tvt,
     xt,
@@ -83,6 +91,8 @@
     core_rs,
     far_ss,
     far_rs,
+    in_sem,
+    side_ss,
 ):
     rows = tv_ref.shape[0]
     heads = step_ref.shape[0]
@@ -102,12 +112,36 @@
     chip = lax.axis_index("head") // 2
     chip_at = [(chip + r) % chips for r in range(chips)]
     far_peer = [2 * at + core_bit for at in chip_at]
-    for _, peer in seq_partner:
+    last = seq_bits - 1
+    n_seq = 2**seq_bits
+    stride = 2 ** (seq_bits // 2)
+    at_seq = lax.axis_index("seq")
+    onward = (at_seq + stride) % n_seq
+    behind = (at_seq + n_seq - stride) % n_seq
+    is_up = at_seq >= n_seq // 2
+    has_next = at_seq + stride < n_seq
+    is_source = jnp.logical_and(at_seq < n_seq // 2, at_seq + stride >= n_seq // 2)
+    for peer in [p for _, p in seq_partner[:last]] + [onward, behind]:
         pl.semaphore_signal(barrier, inc=1, device_id={"seq": peer}, device_id_type=MESH)
     for peer in [core_peer] + far_peer[1:]:
         pl.semaphore_signal(barrier, inc=1, device_id={"head": peer}, device_id_type=MESH)
 
+    pairs = [
+        (decay_hbm, decay_ref),
+        (step_hbm, step_ref),
+        (tv_hbm, tv_ref),
+        (key_hbm, key_ref),
+        (query_hbm, query_ref),
+        (weight_hbm, weight_ref),
+        (gate_hbm, gate_ref),
+        (gain_hbm, gain_ref),
+    ]
+    loads = [
+        pltpu.make_async_copy(src, dst, in_sem.at[i]) for i, (src, dst) in enumerate(pairs)
+    ]
     w_copy = pltpu.make_async_copy(w_hbm, w_ref, w_sem)
+    for load in loads:
+        load.start()
     w_copy.start()
 
     def send(axis, peer, src, dst, ss, rs):
@@ -128,26 +162,52 @@
     def total_copy(d):
         return send("seq", seq_partner[d][1], e_own.at[d], e_got.at[d], e_ss.at[d], e_rs.at[d])
 
+    def turn(g):
+        return at_seq % 2 == g % 2
+
+    def cross_copy(g):
+        return send(
+            "seq", onward, own.at[last, g], got.at[last, g], state_ss.at[last, g], state_rs.at[last, g]
+        )
+
+    def onward_copy(g):
+        return send(
+            "seq", onward, got.at[last, g], got.at[last, g], state_ss.at[last, g], state_rs.at[last, g]
+        )
+
+    def side_copy(g):
+        return send(
+            "seq",
+            seq_partner[0][1],
+            got.at[last, g],
+            got.at[last, g],
+            side_ss.at[g],
+            state_rs.at[last, g],
+        )
+
     u_at = lax.broadcasted_iota(jnp.int32, (rows, rows), 0)
     t_at = lax.broadcasted_iota(jnp.int32, (rows, rows), 1)
+    loads[0].wait()
     decay = decay_ref[...]
     cum = dot(decay, (u_at <= t_at).astype(F32), HIGH)
     to_end = jnp.exp(dot(decay, (u_at > t_at).astype(F32), HIGH))
     total = dot(decay, jnp.ones((rows, LANES), F32), HIGH)
     cum_r[...] = cum
+    loads[1].wait()
     steps = step_ref[...]
     key_scale = steps * to_end
     e_own[0] = jnp.exp(total)
 
-    for j in range(tv_ref.shape[1] // LANES):
-        tvt[pl.ds(j * LANES, LANES), :] = jnp.transpose(
-            tv_ref[:, pl.ds(j * LANES, LANES)].astype(F32)
-        )
-
-    pl.semaphore_wait(barrier, seq_bits + chips)
+    loads[2].wait()
+    loads[3].wait()
+    pl.semaphore_wait(barrier, last + 2 + chips)
     total_copy(0).start()
     keys = key_ref[...]
     for g in range(groups):
+        for j in range(g * span // LANES, (g + 1) * span // LANES):
+            tvt[pl.ds(j * LANES, LANES), :] = jnp.transpose(
+                tv_ref[:, pl.ds(j * LANES, LANES)].astype(F32)
+            )
         parts = []
         for h in range(g * GROUP, (g + 1) * GROUP):
             value = tvt[pl.ds(h * P_SIZE, P_SIZE), :]
@@ -156,6 +216,8 @@
         own[0, g] = dot(jnp.concatenate(parts, axis=0), keys).astype(BF16)
         state_copy(0, g).start()
 
+    for load in loads[4:]:
+        load.wait()
     lift[...] = jnp.exp(cum)
     cum_c[...] = jnp.transpose(cum)
     for l in range(weight_ref.shape[0]):
@@ -171,7 +233,7 @@
     square[...] = jnp.zeros_like(square)
     for j in range(gate_ref.shape[1] // LANES):
         gain_t[pl.ds(j * LANES, LANES), :] = jnp.transpose(
-            jnp.broadcast_to(gain_ref[:, pl.ds(j * LANES, LANES)], (LANES, LANES))
+            jnp.broadcast_to(gain_ref[pl.ds(j * LANES, LANES)].reshape(1, LANES), (LANES, LANES))
         )
 
     def local_part(g):
@@ -200,30 +262,7 @@
             gate = jnp.transpose(gate_ref[:, pl.ds(j * LANES, LANES)].astype(F32))
             silu_t[pl.ds(j * LANES, LANES), :] = gate / (1.0 + jnp.exp(-gate))
 
-    def far_part(d, g):
-        bit, _ = seq_partner[d]
-        up = bit.astype(F32)
-        if g == 0:
-            total_copy(d).wait()
-            mine, theirs = e_own[d], e_got[d]
-            reach = jnp.ones_like(mine) if d == 0 else factor[d]
-            if d + 1 < seq_bits:
-                factor[d + 1] = reach * (up * theirs + (1.0 - up))
-                e_own[d + 1] = mine * theirs
-                total_copy(d + 1).start()
-        state_copy(d, g).wait_recv()
-        if d + 1 < seq_bits:
-            mine, theirs = e_own[d], e_got[d]
-            keep = up + (1.0 - up) * theirs
-            take = up * mine + (1.0 - up)
-            for i in range(GROUP):
-                h = g * GROUP + i
-                at = pl.ds(i * P_SIZE, P_SIZE)
-                own[d + 1, g, at, :] = (
-                    own[d, g, at, :].astype(F32) * keep[h : h + 1, :]
-                    + got[d, g, at, :].astype(F32) * take[h : h + 1, :]
-                ).astype(BF16)
-            state_copy(d + 1, g).start()
+    def add_far(d, g, up):
         reached = dot_nt(got[d, g], query_ref[...])
         for i in range(GROUP):
             h = g * GROUP + i
@@ -234,6 +273,53 @@
                 scale = scale * jnp.concatenate([reach] * tiles, axis=1)
             mixed[at, :] += reached[i * P_SIZE : (i + 1) * P_SIZE] * scale
 
+    def far_part(d, g):
+        bit, _ = seq_partner[d]
+        up = bit.astype(F32)
+        if g == 0:
+            total_copy(d).wait()
+            mine, theirs = e_own[d], e_got[d]
+            reach = jnp.ones_like(mine) if d == 0 else factor[d]
+            factor[d + 1] = reach * (up * theirs + (1.0 - up))
+            if d + 1 < last:
+                e_own[d + 1] = mine * theirs
+                total_copy(d + 1).start()
+        state_copy(d, g).wait_recv()
+        mine, theirs = e_own[d], e_got[d]
+        keep = up + (1.0 - up) * theirs
+        take = up * mine + (1.0 - up)
+        for i in range(GROUP):
+            h = g * GROUP + i
+            at = pl.ds(i * P_SIZE, P_SIZE)
+            own[d + 1, g, at, :] = (
+                own[d, g, at, :].astype(F32) * keep[h : h + 1, :]
+                + got[d, g, at, :].astype(F32) * take[h : h + 1, :]
+            ).astype(BF16)
+        if d + 1 < last:
+            state_copy(d + 1, g).start()
+        else:
+
+            @pl.when(jnp.logical_and(is_source, turn(g)))
+            def _():
+                cross_copy(g).start()
+
+        add_far(d, g, up)
+
+    def last_part(g):
+        @pl.when(is_up)
+        def _():
+            side_copy(g).wait_recv()
+
+            @pl.when(turn(g))
+            def _():
+                side_copy(g).start()
+
+            @pl.when(jnp.logical_and(turn(g), has_next))
+            def _():
+                onward_copy(g).start()
+
+            add_far(last, g, 1.0)
+
     def finish_group(g):
         at = pl.ds(g * span, span)
         gated = mixed[at, :] * silu_t[at, :]
@@ -247,8 +333,10 @@
         for d in range(seq_bits):
             g = k - d
             if 0 <= g < groups:
-                far_part(d, g)
-                if d == seq_bits - 1:
+                if d < last:
+                    far_part(d, g)
+                else:
+                    last_part(g)
                     finish_group(g)
 
     sq_send[0] = square[...]
@@ -341,9 +429,21 @@
             core_copy(r, j).wait_send()
         for r in range(1, chips):
             far_copy(r, j).wait_send()
-    for d in range(seq_bits):
-        for g in range(groups):
+    for g in range(groups):
+        for d in range(last):
             state_copy(d, g).wait_send()
+
+        @pl.when(jnp.logical_and(is_source, turn(g)))
+        def _():
+            cross_copy(g).wait_send()
+
+        @pl.when(jnp.logical_and(is_up, turn(g)))
+        def _():
+            side_copy(g).wait_send()
+
+        @pl.when(jnp.logical_and(jnp.logical_and(is_up, turn(g)), has_next))
+        def _():
+            onward_copy(g).wait_send()
 
 
 def on_device(
@@ -373,8 +473,17 @@
     n_col = model // col
     block = rows // head_devices
     vmem = pl.BlockSpec(memory_space=pltpu.VMEM)
+    hbm = pl.BlockSpec(memory_space=pl.ANY)
     dma = pltpu.SemaphoreType.DMA
     scratch = [
+        pltpu.VMEM((rows, width), BF16),
+        pltpu.VMEM((rows, width), BF16),
+        pltpu.VMEM((rows, n_state), BF16),
+        pltpu.VMEM((rows, n_state), BF16),
+        pltpu.VMEM((heads, rows), F32),
+        pltpu.VMEM((heads, rows), F32),
+        pltpu.VMEM((levels, heads, rows), BF16),
+        pltpu.VMEM((width,), F32),
         pltpu.VMEM((width, model), BF16),
         pltpu.VMEM((width, rows), F32),
         pltpu.VMEM((width, rows), BF16),
@@ -411,18 +520,19 @@
         dma((chips, n_col)),
         dma((chips - 1, n_col)),
         dma((chips - 1, n_col)),
+        dma((8,)),
+        dma((groups,)),
     ]
     return pl.pallas_call(
         functools.partial(
             mixer_kernel, seq_bits, float(width * head_devices), col, group, head_devices
         ),
         out_shape=jax.ShapeDtypeStruct((block, model), BF16),
-        in_specs=[vmem] * 7
-        + [pl.BlockSpec(memory_space=pltpu.SMEM), vmem, pl.BlockSpec(memory_space=pl.ANY)],
+        in_specs=[hbm] * 7 + [pl.BlockSpec(memory_space=pltpu.SMEM), hbm, hbm],
         out_specs=vmem,
         scratch_shapes=scratch,
         compiler_params=pltpu.CompilerParams(
-            collective_id=0, has_side_effects=True, vmem_limit_bytes=48 * 1024 * 1024
+            collective_id=0, has_side_effects=True, vmem_limit_bytes=58 * 1024 * 1024
         ),
         cost_estimate=pl.CostEstimate(
             flops=2 * rows * width * (model + 4 * rows), bytes_accessed=2 * width * model, transcendentals=heads * rows * rows
@@ -437,7 +547,7 @@
         jnp.transpose(log_decay),
         jnp.transpose(level_weight, (2, 1, 0)),
         skip_weight,
-        norm_gain.reshape(1, width),
+        norm_gain,
         out_weight,
     )
 

time: 48.9 us -> 52.8 us (1.080)
  the two profiles are of different devices: /device:TPU:9 before, /device:TPU:27 now
where the time goes in v2:
time: 52.8 us; the launch traced here: 52.7 us
  Pallas kernels  50.9 us (96%)
  local copies, waits for them, and re-layouts  1.72 us (3%)
    pallas_call x1, Pallas kernels, on_device(): pl.pallas_call(functools.partial(mixer_kernel, seq_bits, float(width * he...  50.9 us
    unnamed x1, local copies, waits for them, and re-layouts  1.72 us

profile of v2, /device:TPU:27, one launch (start us, length us, event | category | flops | bytes accessed | tf_op | source)
XLA Modules:
  0.0 52.7 jit_solution(7342274400343270347)
XLA Ops:
  0.0 50.9 %mixer.1 = bf16[64,2560]{1,0:T(8,128)(2,1)} custom-call(bf16[256,1280]{1,0:T(8,128)(2,1)} %tv_hbm.1, bf16[256,1280]{1,0:T(8,128)(2,1)} %gate_hbm.1, bf16[256,128]{1,0:T(8,128)(2,1)} %key_hbm.1, bf16[256,128]{1,0:T(8,128)(2,1)} %query_hbm.1, f32[20,256]{1,0:T(8,128)} %bitcast.4, f32[20,256]{1,0:T(8,128)} %bitcast.5, bf16[12,20,256]{2,1,0:T(8,128)(2,1)} %bitcast.3, ...), custom_call_target="tpu_custom_call" | custom-call | flops 2348810240 | bytes 6553600 | tf_op jit(solution)/shard_map/mixer/pallas_call | solution.py:526
  51.0 1.7 %copy.12 = bf16[64,2560]{1,0:T(8,128)(2,1)} copy(bf16[64,2560]{1,0:T(8,128)(2,1)} %mixer.1) | data formatting | bytes 655360

commit v3 on v2

--- a/solution.py
+++ b/solution.py
@@ -92,7 +92,6 @@
     far_ss,
     far_rs,
     in_sem,
-    side_ss,
 ):
     rows = tv_ref.shape[0]
     heads = step_ref.shape[0]
@@ -114,14 +113,9 @@
     far_peer = [2 * at + core_bit for at in chip_at]
     last = seq_bits - 1
     n_seq = 2**seq_bits
-    stride = 2 ** (seq_bits // 2)
     at_seq = lax.axis_index("seq")
-    onward = (at_seq + stride) % n_seq
-    behind = (at_seq + n_seq - stride) % n_seq
     is_up = at_seq >= n_seq // 2
-    has_next = at_seq + stride < n_seq
-    is_source = jnp.logical_and(at_seq < n_seq // 2, at_seq + stride >= n_seq // 2)
-    for peer in [p for _, p in seq_partner[:last]] + [onward, behind]:
+    for _, peer in seq_partner:
         pl.semaphore_signal(barrier, inc=1, device_id={"seq": peer}, device_id_type=MESH)
     for peer in [core_peer] + far_peer[1:]:
         pl.semaphore_signal(barrier, inc=1, device_id={"head": peer}, device_id_type=MESH)
@@ -162,29 +156,6 @@
     def total_copy(d):
         return send("seq", seq_partner[d][1], e_own.at[d], e_got.at[d], e_ss.at[d], e_rs.at[d])
 
-    def turn(g):
-        return at_seq % 2 == g % 2
-
-    def cross_copy(g):
-        return send(
-            "seq", onward, own.at[last, g], got.at[last, g], state_ss.at[last, g], state_rs.at[last, g]
-        )
-
-    def onward_copy(g):
-        return send(
-            "seq", onward, got.at[last, g], got.at[last, g], state_ss.at[last, g], state_rs.at[last, g]
-        )
-
-    def side_copy(g):
-        return send(
-            "seq",
-            seq_partner[0][1],
-            got.at[last, g],
-            got.at[last, g],
-            side_ss.at[g],
-            state_rs.at[last, g],
-        )
-
     u_at = lax.broadcasted_iota(jnp.int32, (rows, rows), 0)
     t_at = lax.broadcasted_iota(jnp.int32, (rows, rows), 1)
     loads[0].wait()
@@ -200,7 +171,7 @@
 
     loads[2].wait()
     loads[3].wait()
-    pl.semaphore_wait(barrier, last + 2 + chips)
+    pl.semaphore_wait(barrier, seq_bits + chips)
     total_copy(0).start()
     keys = key_ref[...]
     for g in range(groups):
@@ -299,25 +270,16 @@
             state_copy(d + 1, g).start()
         else:
 
-            @pl.when(jnp.logical_and(is_source, turn(g)))
+            @pl.when(at_seq < n_seq // 2)
             def _():
-                cross_copy(g).start()
+                state_copy(last, g).start()
 
         add_far(d, g, up)
 
     def last_part(g):
         @pl.when(is_up)
         def _():
-            side_copy(g).wait_recv()
-
-            @pl.when(turn(g))
-            def _():
-                side_copy(g).start()
-
-            @pl.when(jnp.logical_and(turn(g), has_next))
-            def _():
-                onward_copy(g).start()
-
+            state_copy(last, g).wait_recv()
             add_far(last, g, 1.0)
 
     def finish_group(g):
@@ -433,17 +395,9 @@
         for d in range(last):
             state_copy(d, g).wait_send()
 
-        @pl.when(jnp.logical_and(is_source, turn(g)))
+        @pl.when(at_seq < n_seq // 2)
         def _():
-            cross_copy(g).wait_send()
-
-        @pl.when(jnp.logical_and(is_up, turn(g)))
-        def _():
-            side_copy(g).wait_send()
-
-        @pl.when(jnp.logical_and(jnp.logical_and(is_up, turn(g)), has_next))
-        def _():
-            onward_copy(g).wait_send()
+            state_copy(last, g).wait_send()
 
 
 def on_device(
@@ -521,7 +475,6 @@
         dma((chips - 1, n_col)),
         dma((chips - 1, n_col)),
         dma((8,)),
-        dma((groups,)),
     ]
     return pl.pallas_call(
         functools.partial(

time: 52.8 us -> 39.4 us (0.75)
  the two profiles are of different devices: /device:TPU:27 before, /device:TPU:25 now
where the time goes in v3:
time: 39.4 us; the launch traced here: 39 us
  Pallas kernels  37.3 us (95%)
  local copies, waits for them, and re-layouts  1.72 us (4%)
    pallas_call x1, Pallas kernels, on_device(): pl.pallas_call(functools.partial(mixer_kernel, seq_bits, float(width * he...  37.3 us
    unnamed x1, local copies, waits for them, and re-layouts  1.72 us

profile of v3, /device:TPU:25, one launch (start us, length us, event | category | flops | bytes accessed | tf_op | source)
XLA Modules:
  0.0 39.0 jit_solution(4672011458517017163)
XLA Ops:
  0.0 37.3 %mixer.1 = bf16[64,2560]{1,0:T(8,128)(2,1)} custom-call(bf16[256,1280]{1,0:T(8,128)(2,1)} %tv_hbm.1, bf16[256,1280]{1,0:T(8,128)(2,1)} %gate_hbm.1, bf16[256,128]{1,0:T(8,128)(2,1)} %key_hbm.1, bf16[256,128]{1,0:T(8,128)(2,1)} %query_hbm.1, f32[20,256]{1,0:T(8,128)} %bitcast.4, f32[20,256]{1,0:T(8,128)} %bitcast.5, bf16[12,20,256]{2,1,0:T(8,128)(2,1)} %bitcast.3, ...), custom_call_target="tpu_custom_call" | custom-call | flops 2348810240 | bytes 6553600 | tf_op jit(solution)/shard_map/mixer/pallas_call | solution.py:479
  37.3 1.7 %copy.12 = bf16[64,2560]{1,0:T(8,128)(2,1)} copy(bf16[64,2560]{1,0:T(8,128)(2,1)} %mixer.1) | data formatting | bytes 655360

commit v4 on v3

--- a/solution.py
+++ b/solution.py
@@ -200,7 +200,7 @@
     level = jnp.zeros((LANES, LANES), jnp.int32)
     for shift in range(lane_bits):
         level = level + (apart >= 1 << shift).astype(jnp.int32)
-    level_of[...] = level
+    level_of[...] = level.astype(BF16)
     square[...] = jnp.zeros_like(square)
     for j in range(gate_ref.shape[1] // LANES):
         gain_t[pl.ds(j * LANES, LANES), :] = jnp.transpose(
@@ -221,12 +221,17 @@
                     fade = jnp.exp(jnp.minimum(row - column, 0.0)) * score_t[sub, lanes]
                     if bs == bt:
                         level_now = level_of[...]
-                        weight = jnp.broadcast_to(lw[0, pl.ds(h, 1), lanes], (LANES, LANES))
+                        narrow = [
+                            jnp.broadcast_to(lw[l, pl.ds(h, 1), lanes].astype(BF16), (LANES, LANES))
+                            for l in range(lane_bits + 1)
+                        ]
+                        weight = narrow[0]
                         for l in range(1, lane_bits + 1):
-                            weight = jnp.where(level_now == l, lw[l, pl.ds(h, 1), lanes], weight)
+                            weight = jnp.where(level_now == l, narrow[l], weight)
+                        stack.append(fade.astype(BF16) * weight)
                     else:
                         weight = lw[lane_bits + (bt ^ bs).bit_length(), pl.ds(h, 1), lanes]
-                    stack.append((fade * weight).astype(BF16))
+                        stack.append((fade * weight).astype(BF16))
                 mix = stack[0] if bt == 0 else jnp.concatenate(stack, axis=0)
                 mixed[at, lanes] = dot(x[:, : (bt + 1) * LANES], mix) + skip_ref[h] * tvt[at, lanes]
         for j in range(g * span // LANES, (g + 1) * span // LANES):
@@ -450,7 +455,7 @@
         pltpu.VMEM((rows, heads), F32),
         pltpu.VMEM((heads, rows), F32),
         pltpu.VMEM((rows, rows), F32),
-        pltpu.VMEM((LANES, LANES), jnp.int32),
+        pltpu.VMEM((LANES, LANES), BF16),
         pltpu.VMEM((seq_bits, groups, span, n_state), BF16),
         pltpu.VMEM((seq_bits, groups, span, n_state), BF16),
         pltpu.VMEM((seq_bits, heads, LANES), F32),

time: 39.4 us -> 39.4 us (level)
  no operation moved by 1% of the time
where the time goes in v4:
time: 39.4 us; the launch traced here: 39 us
  Pallas kernels  37.3 us (95%)
  local copies, waits for them, and re-layouts  1.72 us (4%)
    pallas_call x1, Pallas kernels, on_device(): pl.pallas_call(functools.partial(mixer_kernel, seq_bits, float(width * he...  37.3 us
    unnamed x1, local copies, waits for them, and re-layouts  1.72 us

profile of v4, /device:TPU:25, one launch (start us, length us, event | category | flops | bytes accessed | tf_op | source)
XLA Modules:
  0.0 39.0 jit_solution(10037843582800928752)
XLA Ops:
  0.0 37.3 %mixer.1 = bf16[64,2560]{1,0:T(8,128)(2,1)} custom-call(bf16[256,1280]{1,0:T(8,128)(2,1)} %tv_hbm.1, bf16[256,1280]{1,0:T(8,128)(2,1)} %gate_hbm.1, bf16[256,128]{1,0:T(8,128)(2,1)} %key_hbm.1, bf16[256,128]{1,0:T(8,128)(2,1)} %query_hbm.1, f32[20,256]{1,0:T(8,128)} %bitcast.4, f32[20,256]{1,0:T(8,128)} %bitcast.5, bf16[12,20,256]{2,1,0:T(8,128)(2,1)} %bitcast.3, ...), custom_call_target="tpu_custom_call" | custom-call | flops 2348810240 | bytes 6553600 | tf_op jit(solution)/shard_map/mixer/pallas_call | solution.py:484
  37.3 1.7 %copy.12 = bf16[64,2560]{1,0:T(8,128)(2,1)} copy(bf16[64,2560]{1,0:T(8,128)(2,1)} %mixer.1) | data formatting | bytes 655360

commit v5 on v3

--- a/solution.py
+++ b/solution.py
@@ -274,8 +274,6 @@
             def _():
                 state_copy(last, g).start()
 
-        add_far(d, g, up)
-
     def last_part(g):
         @pl.when(is_up)
         def _():
@@ -289,17 +287,20 @@
         gain = jnp.concatenate([gain_t[at, :]] * tiles, axis=1)
         feat[:, at] = jnp.transpose(gated * gain).astype(BF16)
 
-    for k in range(groups + seq_bits):
+    lag = max(3, last + 1)
+    for k in range(groups + lag):
         if k < groups:
             local_part(k)
-        for d in range(seq_bits):
-            g = k - d
-            if 0 <= g < groups:
-                if d < last:
+        for d in range(last):
+            for g in (2 * (k - d), 2 * (k - d) + 1):
+                if 0 <= g < groups:
                     far_part(d, g)
-                else:
-                    last_part(g)
-                    finish_group(g)
+        if k >= lag:
+            g = k - lag
+            for d in range(last):
+                add_far(d, g, seq_partner[d][0].astype(F32))
+            last_part(g)
+            finish_group(g)
 
     sq_send[0] = square[...]
     sq_core = send("head", core_peer, sq_send.at[0], sq_got.at[0], sq_ss.at[0], sq_rs.at[0])

time: 39.4 us -> 40.3 us (1.023)
  Pallas kernels: 37.3 us -> 38.4 us
    pallas_call x1, Pallas kernels: 37.3 us -> 38.4 us  [on_device(): pl.pallas_call(functools.partial(mixer_kernel, seq_bits, float(width * he...]
where the time goes in v5:
time: 40.3 us; the launch traced here: 40.1 us
  Pallas kernels  38.4 us (95%)
  local copies, waits for them, and re-layouts  1.72 us (4%)
    pallas_call x1, Pallas kernels, on_device(): pl.pallas_call(functools.partial(mixer_kernel, seq_bits, float(width * he...  38.4 us
    unnamed x1, local copies, waits for them, and re-layouts  1.72 us

profile of v5, /device:TPU:25, one launch (start us, length us, event | category | flops | bytes accessed | tf_op | source)
XLA Modules:
  0.0 40.1 jit_solution(12913852911594552170)
XLA Ops:
  0.0 38.4 %mixer.1 = bf16[64,2560]{1,0:T(8,128)(2,1)} custom-call(bf16[256,1280]{1,0:T(8,128)(2,1)} %tv_hbm.1, bf16[256,1280]{1,0:T(8,128)(2,1)} %gate_hbm.1, bf16[256,128]{1,0:T(8,128)(2,1)} %key_hbm.1, bf16[256,128]{1,0:T(8,128)(2,1)} %query_hbm.1, f32[20,256]{1,0:T(8,128)} %bitcast.4, f32[20,256]{1,0:T(8,128)} %bitcast.5, bf16[12,20,256]{2,1,0:T(8,128)(2,1)} %bitcast.3, ...), custom_call_target="tpu_custom_call" | custom-call | flops 2348810240 | bytes 6553600 | tf_op jit(solution)/shard_map/mixer/pallas_call | solution.py:480
  38.4 1.7 %copy.12 = bf16[64,2560]{1,0:T(8,128)(2,1)} copy(bf16[64,2560]{1,0:T(8,128)(2,1)} %mixer.1) | data formatting | bytes 655360
